TPU v7x, 32 devices: a whole 2x2x4 slice. The times are simulated.
32 devices in a mesh: groups: 2 (over y), ctx: 4 (over z), tp: 4 (over x, core).
Axes of the slice: x: 2, y: 2, z: 4, core: 2. Of those that a mesh axis runs over, the one named last changes fastest.
Arguments:
- x_in: bfloat16 [4096, 4096], P(('groups', 'ctx'), 'tp'), parts along dimension 0, may hold values from -6 to 6
- z_in: bfloat16 [4096, 4096], P(('groups', 'ctx'), 'tp'), parts along dimension 0, may hold values from -6 to 6
- b_in: bfloat16 [4096, 512], P(('groups', 'ctx'), 'tp'), parts along dimension 0, may hold values from -6 to 6
- c_in: bfloat16 [4096, 512], P(('groups', 'ctx'), 'tp'), parts along dimension 0, may hold values from -6 to 6
- dt_in: bfloat16 [4096, 64], P(('groups', 'ctx'), 'tp'), parts along dimension 0, may hold values from -4 to 14
- conv_x: bfloat16 [4, 4096], P(None, 'tp'), may hold values from -3 to 3
- conv_bc: bfloat16 [2, 4, 512], P(None, None, 'tp'), may hold values from -3 to 3
- dt_bias: float32 [64], P('tp'), may hold values from -13 to -2
- a_log: float32 [64], P('tp'), may hold values from -0.7 to 0.4
- d_skip: float32 [64], P('tp'), may hold values from 0.5 to 1.5
- norm_gain: bfloat16 [4096], P('tp'), may hold values from 0.5 to 1.5
- out_weight: bfloat16 [4096, 4096], P('ctx', 'tp'), may hold values from -0.09375 to 0.09375
Outputs:
- mixed: bfloat16 [4096, 4096], P(('groups', 'ctx'), 'tp'), parts along dimension 0
There are 2 independent parts, one for each index of `groups`. A program takes and returns all parts, laid end to end along the dimension named above; an argument that names none is the same for every part. Nothing has to cross between parts.
All inputs are finite; a program needn't handle non-finite values.
Results may differ from a plain program's by a relative error of at most 0.0059.
Values may be sent and summed in bfloat16 or wider, within the bound.
A program may use at most 128 MiB of HBM per device.

v0:
```python
import jax
import jax.numpy as jnp
from jax import lax
from jax.sharding import PartitionSpec as P

STATE = 128
SPAN = 256


EPS = 1e-05


def entering_2(value, axis, join, neutral):
    count, mine = (lax.axis_size(axis), lax.axis_index(axis))
    pieces = jax.tree.map(lambda part: lax.all_gather(part, axis), value)
    total = jax.tree.map(
        lambda part, zero: jnp.full_like(part, 0) + jnp.asarray(zero, part.dtype), value, neutral
    )

    def hop(position, total):
        longer = join(total, jax.tree.map(lambda part: part[position], pieces))
        return jax.tree.map(lambda new, old: jnp.where(position < mine, new, old), longer, total)

    return lax.fori_loop(0, count - 1, hop, total)


def from_behind(block, axis, distance):
    devices = range(lax.axis_size(axis))
    route = [(i - distance, i) for i in devices if i - distance in devices]
    return lax.ppermute(block, axis, route)


def causal_conv(extended, taps, length):
    summed = jnp.zeros((length, extended.shape[1]), jnp.float32)
    for kernel_tap in range(taps.shape[0]):
        summed = summed + extended[kernel_tap : kernel_tap + length].astype(jnp.float32) * taps[
            kernel_tap
        ].astype(jnp.float32)
    return jax.nn.silu(summed).astype(jnp.bfloat16)


def span_parts(x_rows, b_rows, c_rows, step_span, decay_rate, groups):
    length = x_rows.shape[0]
    head_count = step_span.shape[1]
    per_group = head_count // groups
    state_size = b_rows.shape[1] // groups
    b_groups = b_rows.reshape(length, groups, state_size)
    c_groups = c_rows.reshape(length, groups, state_size)
    x_heads = x_rows.reshape(length, head_count, -1)
    cumulative = jnp.cumsum(step_span * decay_rate[None, :], axis=0)
    scores = jnp.einsum("tgn,sgn->gts", c_groups, b_groups, preferred_element_type=jnp.float32)
    positions = jnp.arange(length)
    causal = positions[:, None] >= positions[None, :]
    transposed = cumulative.T
    gaps = jnp.where(causal[None], transposed[:, :, None] - transposed[:, None, :], -1e30)
    mixing = (
        jnp.repeat(scores, per_group, axis=0) * jnp.exp(gaps) * step_span.T[:, None, :]
    ).astype(jnp.bfloat16)
    diagonal_part = jnp.einsum("hts,shp->thp", mixing, x_heads, preferred_element_type=jnp.float32)
    to_end = jnp.exp(cumulative[-1][None, :] - cumulative) * step_span
    weighted = (x_heads.astype(jnp.float32) * to_end[:, :, None]).astype(jnp.bfloat16)
    b_heads = jnp.repeat(b_groups, per_group, axis=1)
    local_state = jnp.einsum("shp,shn->hpn", weighted, b_heads, preferred_element_type=jnp.float32)
    return (diagonal_part.reshape(length, -1), local_state, cumulative)


def carried(c_rows, cumulative, entering, groups):
    length = c_rows.shape[0]
    head_count = cumulative.shape[1]
    state_size = entering.shape[2]
    c_heads = jnp.repeat(
        c_rows.reshape(length, groups, state_size), head_count // groups, axis=1
    ).astype(jnp.float32)
    summed = jnp.einsum("thn,hpn->thp", c_heads, entering, precision=lax.Precision.HIGHEST)
    return (summed * jnp.exp(cumulative)[:, :, None]).reshape(length, -1)


def finish(ssd_part, x_rows, gate_rows, d_skip, norm_gain, groups):
    length, inner_here = x_rows.shape
    head_count = d_skip.shape[0]
    skip_term = (
        x_rows.astype(jnp.float32).reshape(length, head_count, -1) * d_skip[None, :, None]
    ).reshape(length, inner_here)
    gated = (ssd_part + skip_term) * jax.nn.silu(gate_rows.astype(jnp.float32))
    grouped = gated.reshape(length, groups, -1)
    scale = lax.rsqrt(jnp.mean(grouped * grouped, axis=2, keepdims=True) + EPS)
    return ((grouped * scale).reshape(length, inner_here) * norm_gain.astype(jnp.float32)).astype(
        jnp.bfloat16
    )


def chain(decays, states):

    def combine(earlier, later):
        return (earlier[0] * later[0], later[0][:, None, None] * earlier[1] + later[1])

    identity = (jnp.ones_like(decays), jnp.zeros_like(states))
    return entering_2((decays, states), "ctx", combine, identity)


def shards(
    x_in, z_in, b_in, c_in, dt_in, conv_x, conv_bc, dt_bias, a_log, d_skip, norm_gain, out_weight
):
    local_tokens = x_in.shape[0]
    rim_rows = conv_x.shape[0] - 1
    head_count = dt_in.shape[1]
    groups_here = b_in.shape[1] // STATE
    span_count = local_tokens // SPAN
    prev_x, prev_b, prev_c = from_behind(
        (
            x_in[local_tokens - rim_rows :],
            b_in[local_tokens - rim_rows :],
            c_in[local_tokens - rim_rows :],
        ),
        "ctx",
        1,
    )
    xs = causal_conv(jnp.concatenate([prev_x, x_in], 0), conv_x, local_tokens)
    bs = causal_conv(jnp.concatenate([prev_b, b_in], 0), conv_bc[0], local_tokens)
    cs = causal_conv(jnp.concatenate([prev_c, c_in], 0), conv_bc[1], local_tokens)
    step_size = jax.nn.softplus(dt_in.astype(jnp.float32) + dt_bias[None, :])
    decay_rate = -jnp.exp(a_log)
    head_width = x_in.shape[1] // head_count

    def advance(carry, span_index):
        running, offset = carry
        first_row = span_index * SPAN

        def take_rows(array):
            return lax.dynamic_slice_in_dim(array, first_row, SPAN, 0)

        c_rows = take_rows(cs)
        diagonal_part, local_state, cumulative = span_parts(
            take_rows(xs), take_rows(bs), c_rows, take_rows(step_size), decay_rate, groups_here
        )
        diagonal_part = diagonal_part + carried(c_rows, cumulative, running, groups_here)
        following = jnp.exp(cumulative[-1])[:, None, None] * running + local_state
        return (
            (following, offset + cumulative[-1]),
            (diagonal_part, cumulative, cumulative + offset[None, :], local_state),
        )

    start_state = jnp.zeros((head_count, head_width, STATE), jnp.float32)
    start_offset = jnp.zeros((head_count,), jnp.float32)
    (device_state, device_log), (partial_out, span_cums, through, span_states) = lax.scan(
        advance, (start_state, start_offset), jnp.arange(span_count, dtype=jnp.int32)
    )
    partial_out = partial_out.reshape(local_tokens, -1)
    prefix_state = chain(jnp.exp(device_log), device_state)[1]
    ssd_part = partial_out + carried(
        cs, through.reshape(local_tokens, head_count), prefix_state, groups_here
    )
    normed = finish(ssd_part, xs, z_in, d_skip, norm_gain, groups_here)
    gathered = lax.all_gather(normed, "tp", axis=1, tiled=True)
    weight_full = lax.all_gather(out_weight, "ctx", axis=0, tiled=True)
    mixed = jnp.dot(gathered, weight_full, preferred_element_type=jnp.float32)
    return mixed.astype(jnp.bfloat16)


def solution(mesh):
    return jax.shard_map(
        shards,
        mesh=mesh,
        in_specs=(
            P(("groups", "ctx"), "tp"),
            P(("groups", "ctx"), "tp"),
            P(("groups", "ctx"), "tp"),
            P(("groups", "ctx"), "tp"),
            P(("groups", "ctx"), "tp"),
            P(None, "tp"),
            P(None, None, "tp"),
            P("tp"),
            P("tp"),
            P("tp"),
            P("tp"),
            P("ctx", "tp"),
        ),
        out_specs=P(("groups", "ctx"), "tp"),
        check_vma=False,
    )
```

profile of v0, /device:TPU:26, one launch (start us, length us, event | category | flops | bytes accessed | tf_op | source)
XLA Modules:
  0.0 304.5 jit_solution(9660425801306067295)
XLA Ops:
  6.5 0.7 slice.117
  7.2 1.3 collective-permute-start.2
  8.5 0.7 slice.109
  9.2 1.3 collective-permute-start.1
  10.5 0.7 slice.101
  11.2 1.3 collective-permute-start
  12.5 0.9 bitcast_convert_fusion.3
  13.4 0.9 slice_convert_fusion.3
  14.2 0.8 compare_select_fusion
  15.1 0.7 exponential_negate_fusion
  15.7 1.3 multiply_convert_fusion.8
  17.1 2.0 multiply_convert_fusion.9
  19.1 4.3 %multiply_convert_fusion.7 = bf16[512,1024]{1,0:T(8,128)(2,1)} fusion(bf16[512,1024]{1,0:T(8,128)(2,1)} %param.16, bf16[3,1024]{1,0:T(4,128)(2,1)S(1)} %collective-permute-done, f32[1024]{0:T(1024)S(1)} %bitcast.144, f32[1024]{0:T(1024)S(1)} %bitcast.145, f32[1024]{0:T(1024)S(1)} %bitcast.143, f32[1024]{0:T(1024)S(1)} %bitcast.142), kind=kLoop, calls=%fused_computation.53 | loop fusion | flops 13107200 | bytes 2119680 | tf_op jit(solution)/shard_map/convert_element_type | solution.py:39
  23.4 18.3 %while.31 = (s32[]{:T(128)}, f32[16,64,128]{2,1,0:T(8,128)S(1)}, f32[16]{0:T(128)S(1)}, f32[2,256,1024]{2,1,0:T(8,128)}, f32[2,256,16]{1,2,0:T(8,128)S(1)}, /*in...) while((s32[]{:T(128)}, f32[16,64,128]{2,1,0:T(8,128)S(1)}, ...), condition=%wide.region_3.4_spmd.clone, body=%wide.region_0.3_spmd.clone.sunk | while | flops 628449408 | bytes 13537655 | solution.py:145
  23.4 0.6 dynamic_slice.57
  24.8 0.6 reduce-window.14
  25.4 0.2 slice_reduce_fusion.4
  25.6 0.1 copy_bitcast_fusion.5
  25.6 0.2 slice_reduce_fusion.5
  25.8 0.1 dynamic-slice_bitcast_fusion.4
  25.9 0.9 constant_dynamic-slice_fusion.6
  26.8 0.2 fusion.59
  27.0 1.1 constant_dynamic-slice_fusion.5
  28.1 0.2 copy.67
  28.3 1.2 fusion.60
  29.5 1.2 fusion.61
  30.7 0.3 copy.68
  31.1 1.1 constant_dynamic-update-slice_fusion.2
  32.2 0.3 convolution_add_fusion.2
  32.5 0.1 bitcast_dynamic-update-slice_fusion.2
  32.6 0.6 dynamic_slice.57
  33.9 0.6 reduce-window.14
  34.5 0.2 slice_reduce_fusion.4
  34.7 0.1 copy_bitcast_fusion.5
  34.8 0.2 slice_reduce_fusion.5
  35.0 0.1 dynamic-slice_bitcast_fusion.4
  35.1 0.9 constant_dynamic-slice_fusion.6
  35.9 0.2 fusion.59
  36.1 1.1 constant_dynamic-slice_fusion.5
  37.2 0.2 copy.67
  37.4 1.2 fusion.60
  38.7 1.2 fusion.61
  39.9 0.3 copy.68
  40.2 1.1 constant_dynamic-update-slice_fusion.2
  41.3 0.3 convolution_add_fusion.2
  41.6 0.1 bitcast_dynamic-update-slice_fusion.2
  41.7 0.8 copy-done
  42.8 0.6 dynamic-slice
  43.9 0.1 exponential_dynamic-update-slice_fusion
  44.0 13.3 %all-reduce = f32[64]{0:T(128)S(1)} all-reduce(f32[64]{0:T(128)S(1)} %exponential_dynamic-update-slice_fusion), channel_id=2, replica_groups=mesh['groups'=2,'ctx'=4,'tp'=4] {'ctx'}, use_global_device_ids=true, to_apply=%add | all-reduce | flops 64 | bytes 512
  57.4 0.1 reshape.224
  57.5 33.5 %all-gather.10.cloned.1.call-done = f32[64,64,128]{2,1,0:T(8,128)} async-done(((f32[16,64,128]{2,1,0:T(8,128)}), f32[64,64,128]{2,1,0:T(8,128)}) %all-gather.10.cloned.1.call-update) | async-done | bytes 2097168 | tf_op jit(solution)/shard_map/all_gather | solution.py:15
  91.0 3.6 %while.32 = (s32[]{:T(128)}, f32[16,64,128]{2,1,0:T(8,128)S(1)}, s32[]{:T(128)}, f32[4,16]{1,0:T(4,128)S(1)}, f32[4,16,64,128]{3,2,1,0:T(8,128)}, /*index=5*/s32[]{:T(128)}, s32[]{:T(128)}) while((s32[]{:T(128)}, f32[16,64,128]{2,1,0:T(8,128)S(1)}, s32[]{:T(128)}, f32[4,16]{1,0:T(4,128)S(1)}, f32[4,16,64,128]{3,2,1,0:T(8,128)}, ...), condition=%wide.region_5.6_spmd.clone, body=%wide.region_4.5_spmd.clone.sunk | while | flops 524292 | bytes 1573161 | solution.py:24
  91.0 1.2 fusion.62
  92.2 1.2 fusion.62
  93.4 1.2 fusion.62
  94.6 2.3 bitcast_multiply_fusion
  96.9 1.9 copy.41
  98.8 3.8 %multiply_reduce_fusion = (f32[512]{0:T(512)S(1)}, f32[512,1024]{1,0:T(8,128)S(1)}) fusion(bf16[512,1024]{1,0:T(8,128)(2,1)} %param.17, f32[1024]{0:T(1024)S(1)} %mul.289, bf16[512,1024]{1,0:T(8,128)(2,1)} %multiply_convert_fusion.7, f32[512,1024]{1,0:T(8,128)} %copy.41, f32[2,256,1024]{2,1,0:T(8,128)} %get-tuple-element.159), kind=kLoop, calls=%fused_computation.52 | loop fusion | flops 6290944 | bytes 8394752 | tf_op jit(solution)/shard_map/reduce_sum | solution.py:86
  102.6 1.2 multiply_convert_fusion.6
  103.9 0.7 all-gather.8.cloned.1.call-update
  104.6 33.9 %all-gather.6.cloned.1.call-done = bf16[512,4096]{1,0:T(8,128)(2,1)} async-done(((bf16[512,1024]{1,0:T(8,128)(2,1)}), bf16[512,4096]{1,0:T(8,128)(2,1)}) %all-gather.6.cloned.1.call-update) | async-done | bytes 4194320 | tf_op jit(solution)/shard_map/all_gather | solution.py:154
  138.5 149.4 %all-gather.8.cloned.1.call-done = bf16[4096,1024]{1,0:T(8,128)(2,1)} async-done(((bf16[1024,1024]{1,0:T(8,128)(2,1)}), bf16[4096,1024]{1,0:T(8,128)(2,1)}) %all-gather.8.cloned.1.call-update) | async-done | bytes 8388624 | tf_op jit(solution)/shard_map/all_gather | solution.py:155
  287.9 10.1 %convolution_convert_fusion = bf16[512,1024]{1,0:T(8,128)(2,1)} fusion(bf16[512,4096]{1,0:T(8,128)(2,1)} %all-gather.6.cloned.1.call-done, bf16[4096,1024]{1,0:T(8,128)(2,1)} %all-gather.8.cloned.1.call-done), kind=kOutput, calls=%fused_computation.54 | convolution fusion | flops 4295491584 | bytes 13631488 | tf_op jit(solution)/shard_map/dot_general | solution.py:156
  (41 shorter events, 0.6 us)
Async XLA Ops:
  6.5 84.5 %all-gather.10.cloned.1.call-start = ((), (), s32[]{:S(2)}) async-start(), calls=%async_computation.2 | async-start | bytes 2621440 | tf_op jit(solution)/shard_map/all_gather | solution.py:15
  7.2 8.5 %collective-permute-start.2 = (bf16[3,128]{1,0:T(4,128)(2,1)S(1)}, bf16[3,128]{1,0:T(4,128)(2,1)S(1)}, u32[]{:S(2)}, u32[]{:S(2)}) collective-permute-start(bf16[3,128]{1,0:T(4,128)(2,1)S(1)} %slice.117), channel_id=1, source_target_pairs={{0,4},{4,8},{8,12},{1,5},{5,9},{9,13},{2,6},{6,10},{10,14},{3,7},{... | collective-permute-start | bytes 2312 | tf_op jit(solution)/shard_map/ppermute | solution.py:30
  9.2 7.9 %collective-permute-start.1 = (bf16[3,128]{1,0:T(4,128)(2,1)S(1)}, bf16[3,128]{1,0:T(4,128)(2,1)S(1)}, u32[]{:S(2)}, u32[]{:S(2)}) collective-permute-start(bf16[3,128]{1,0:T(4,128)(2,1)S(1)} %slice.109), channel_id=1, source_target_pairs={{0,4},{4,8},{8,12},{1,5},{5,9},{9,13},{2,6},{6,10},{10,14},{3,7},{... | collective-permute-start | bytes 2312 | tf_op jit(solution)/shard_map/ppermute | solution.py:30
  11.2 7.9 %collective-permute-start = (bf16[3,1024]{1,0:T(4,128)(2,1)S(1)}, bf16[3,1024]{1,0:T(4,128)(2,1)S(1)}, u32[]{:S(2)}, u32[]{:S(2)}) collective-permute-start(bf16[3,1024]{1,0:T(4,128)(2,1)S(1)} %slice.101), channel_id=1, source_target_pairs={{0,4},{4,8},{8,12},{1,5},{5,9},{9,13},{2,6},{6,10},{10,14},{3,7},{... | collective-permute-start | bytes 18440 | tf_op jit(solution)/shard_map/ppermute | solution.py:30
  23.4 19.2 %copy-start.2 = (f32[16]{0:T(128)S(1)}, f32[16]{0:T(128)}, u32[]{:S(2)}) copy-start(f32[16]{0:T(128)} %param.25) | copy-start | bytes 196
  23.4 19.4 %copy-start.1 = (bf16[1024]{0:T(1024)(128)(2,1)S(1)}, bf16[1024]{0:T(1024)(128)(2,1)}, u32[]{:S(2)}) copy-start(bf16[1024]{0:T(1024)(128)(2,1)} %param.26) | copy-start | bytes 6148
  23.4 19.4 %copy-start.3 = (u32[32]{0:T(128)S(1)}, u32[32]{0:T(128)}, u32[]{:S(2)}) copy-start(u32[32]{0:T(128)} %constant.72) | copy-start | bytes 388
  41.7 0.8 copy-start
  42.6 96.0 %all-gather.6.cloned.1.call-start = ((), (), s32[]{:S(2)}) async-start(), calls=%async_computation | async-start | bytes 5242880 | tf_op jit(solution)/shard_map/all_gather | solution.py:154
  103.9 184.0 %all-gather.8.cloned.1.call-start = ((), (), s32[]{:S(2)}) async-start(), calls=%async_computation.1 | async-start | bytes 10485760 | tf_op jit(solution)/shard_map/all_gather | solution.py:155
Sparse Core Ops, SparseCore 0:
  42.7 48.2 all-gather.9
  104.0 34.4 all-gather.5
  140.1 147.7 all-gather.7
where the time goes:
time: 310 us; the launch traced here: 305 us
  waiting for transfers between devices  218 us (70%)
  other arithmetic  21.4 us (7%)
  matrix products  18.2 us (6%)
  local copies, waits for them, and re-layouts  14.9 us (5%)
  between operations  13.8 us (4%)
  blocking collectives  13.3 us (4%)
  starting transfers between devices  3.93 us (1%)
    all_gather x1, waiting for transfers between devices, shards(): weight_full = lax.all_gather(out_weight, 'ctx', axis=0, tiled=True)  149 us
    all_gather x1, waiting for transfers between devices, shards(): gathered = lax.all_gather(normed, 'tp', axis=1, tiled=True)  33.9 us
    all_gather x1, waiting for transfers between devices, entering_2(): pieces = jax.tree.map(lambda part: lax.all_gather(part, axis), value)  33.5 us
    unnamed x1, blocking collectives  13.3 us
    dot_general x1, matrix products, shards(): mixed = jnp.dot(gathered, weight_full, preferred_element_type=jnp.float32)  10.1 us
    convert_element_type x3, other arithmetic, causal_conv(): return jax.nn.silu(summed).astype(jnp.bfloat16)  7.65 us
  transfers between devices with their start and end apart: 6, of which 3 were waited for; matrix products, arithmetic and copies ran while one was open for 3% of the time, Pallas kernels for 0%

commit v1 on v0

v1 whole, which is shorter than its diff:
```python
import functools
import jax
import jax.numpy as jnp
from jax import lax
from jax.experimental import pallas as pl
from jax.experimental.pallas import tpu as pltpu
from jax.sharding import PartitionSpec as P

STATE = 128
SPAN = 256
EPS = 1e-05
RIM = 16
TILE = 256
MESH = pl.DeviceIdType.MESH
F32 = jnp.float32
BF16 = jnp.bfloat16


def dot(a, b):
    return jnp.dot(a, b, preferred_element_type=F32)


def silu(v):
    return v / (1.0 + jnp.exp(-v))


def spread(value, table):
    high = value.astype(BF16)
    low = (value - high.astype(F32)).astype(BF16)
    return dot(high, table) + dot(low, table)


def kernel(
    n, chunks,
    x_ref, z_ref, b_ref, c_ref, dt_ref, conv_ref, convbc_ref, bias_ref, alog_ref, skip_ref, gain_ref, w_ref,
    o_ref,
    wfull, nall, xe, xs, bs, cs, ssd, state0, state1, entering, outgoing, halo_x, halo_b, halo_c,
    own_sem, halo_send, halo_recv, chain_send, chain_recv,
    right_send, right_recv, left_send, left_recv,
    yr_send, yr_recv, yl_send, yl_recv,
    tp_send, tp_recv,
):
    g = lax.axis_index("groups")
    me = lax.axis_index("ctx")
    p = lax.axis_index("tp")
    other = 1 - g
    near = p + 1 - 2 * lax.rem(p, 2)
    far = lax.rem(p + 2, 4)
    rows, inner = x_ref.shape
    heads = dt_ref.shape[1]
    width = inner // heads
    spans = rows // SPAN
    depth = w_ref.shape[0]
    half = depth // 2
    piece = half // chunks
    has_left, has_right = me > 0, me < n - 1

    barrier = pltpu.get_barrier_semaphore()
    for device in ({"groups": other}, {"tp": near}, {"tp": far}):
        pl.semaphore_signal(barrier, inc=1, device_id=device, device_id_type=MESH)

    @pl.when(has_left)
    def _():
        pl.semaphore_signal(barrier, inc=1, device_id={"ctx": me - 1}, device_id_type=MESH)

    @pl.when(has_right)
    def _():
        pl.semaphore_signal(barrier, inc=1, device_id={"ctx": me + 1}, device_id_type=MESH)

    pl.semaphore_wait(barrier, 3 + has_left.astype(jnp.int32) + has_right.astype(jnp.int32))

    def remote(src, dst, send, recv, device):
        return pltpu.make_async_remote_copy(
            src_ref=src, dst_ref=dst, send_sem=send, recv_sem=recv, device_id=device, device_id_type=MESH
        )

    def halo(i):
        src = (x_ref, b_ref, c_ref)[i].at[pl.ds(rows - RIM, RIM)]
        dst = (halo_x, halo_b, halo_c)[i]
        return remote(src, dst, halo_send.at[i], halo_recv.at[i], {"ctx": me + 1})

    @pl.when(has_right)
    def _():
        for i in range(3):
            halo(i).start()

    def strip(block, part, k):
        return pl.ds(pl.multiple_of(block * depth + part * half + k * piece, 16), piece)

    def own_strip(k):
        return pl.ds(pl.multiple_of(g * half + k * piece, 16), piece)

    def go_right(s, k):
        src = w_ref.at[own_strip(k)] if isinstance(s, int) and s == 0 else wfull.at[strip(me - s, g, k)]
        return remote(
            src, wfull.at[strip(me - s, g, k)],
            right_send.at[s * chunks + k], right_recv.at[s * chunks + k], {"ctx": me + 1},
        )

    def go_left(s, k):
        src = w_ref.at[own_strip(k)] if isinstance(s, int) and s == 0 else wfull.at[strip(me + s, g, k)]
        return remote(
            src, wfull.at[strip(me + s, g, k)],
            left_send.at[s * chunks + k], left_recv.at[s * chunks + k], {"ctx": me - 1},
        )

    def arrival(s, k, from_left):
        at = strip(me - s if from_left else me + s, g, k)
        send, recv = (right_send, right_recv) if from_left else (left_send, left_recv)
        spot = (s - 1) * chunks + k
        return remote(
            wfull.at[at], wfull.at[at], send.at[spot], recv.at[spot], {"ctx": me}
        )

    def across(s, k, from_left, part):
        at = strip(me - s if from_left else me + s, part, k)
        send, recv = (yr_send, yr_recv) if from_left else (yl_send, yl_recv)
        spot = (s - 1) * chunks + k
        return remote(wfull.at[at], wfull.at[at], send.at[spot], recv.at[spot], {"groups": other})

    for k in range(chunks):

        @pl.when(has_right)
        def _():
            go_right(0, k).start()

        @pl.when(has_left)
        def _():
            go_left(0, k).start()

    own_copy = pltpu.make_async_copy(
        w_ref, wfull.at[pl.ds(pl.multiple_of(me * depth, 16), depth)], own_sem
    )
    own_copy.start()

    def relay(s, k):
        @pl.when(me - s >= 0)
        def _():
            arrival(s, k, True).wait_recv()

            @pl.when(has_right)
            def _():
                go_right(s, k).start()

            across(s, k, True, g).start()

        @pl.when(me + s < n)
        def _():
            arrival(s, k, False).wait_recv()

            @pl.when(has_left)
            def _():
                go_left(s, k).start()

            across(s, k, False, g).start()

    events = [(s, k) for s in range(1, min(n, 4)) for k in range(chunks)]

    def next_relay():
        if events:
            relay(*events.pop(0))

    @pl.when(jnp.logical_not(has_left))
    def _():
        halo_x[...] = jnp.zeros_like(halo_x)
        halo_b[...] = jnp.zeros_like(halo_b)
        halo_c[...] = jnp.zeros_like(halo_c)

    @pl.when(has_left)
    def _():
        for i in range(3):
            halo(i).wait_recv()

    def conv(src, rim, taps, dst, columns):
        xe[0:8] = rim[:, columns].astype(F32)[RIM - 8 :]
        xe[8 : 8 + rows] = src[:, columns].astype(F32)
        weights = taps(columns).astype(F32)
        for first in range(0, rows, 128):
            total = xe[first + 5 : first + 5 + 128] * weights[0:1]
            for tap in range(1, 4):
                total = total + xe[first + 5 + tap : first + 5 + tap + 128] * weights[tap : tap + 1]
            dst[first : first + 128, columns] = silu(total).astype(BF16)

    every = pl.ds(0, STATE)
    conv(b_ref, halo_b, lambda cols: convbc_ref[0, :, cols], bs, every)
    conv(c_ref, halo_c, lambda cols: convbc_ref[1, :, cols], cs, every)

    @pl.loop(0, inner // STATE)
    def _(tile):
        columns = pl.ds(pl.multiple_of(tile * STATE, STATE), STATE)
        conv(x_ref, halo_x, lambda cols: conv_ref[:, cols], xs, columns)

    raw = dt_ref[...].astype(F32) + bias_ref[...]
    step = jnp.maximum(raw, 0.0) + jnp.log1p(jnp.exp(-jnp.abs(raw)))
    log_decay = -jnp.exp(alog_ref[...]) * step
    t_at = lax.broadcasted_iota(jnp.int32, (SPAN, SPAN), 0)
    s_at = lax.broadcasted_iota(jnp.int32, (SPAN, SPAN), 1)
    causal = t_at >= s_at
    lower = causal.astype(F32)
    eye = (
        lax.broadcasted_iota(jnp.int32, (heads, heads), 0) == lax.broadcasted_iota(jnp.int32, (heads, heads), 1)
    ).astype(F32)

    def turned(value):
        return lax.dot_general(
            eye, value, (((1,), (1,)), ((), ())), precision=lax.Precision.HIGHEST, preferred_element_type=F32
        )

    def table(tile):
        channel = lax.broadcasted_iota(jnp.int32, (heads, TILE), 1) + tile * TILE
        first = lax.broadcasted_iota(jnp.int32, (heads, TILE), 0) * width
        return jnp.logical_and(channel >= first, channel < first + width).astype(BF16)

    tiles = inner // TILE
    tables = [table(tile) for tile in range(tiles)]
    states = (state0, state1)
    steps, cums, ends = [], [], []
    for span in range(spans):
        at = slice(span * SPAN, (span + 1) * SPAN)
        step_here = step[at]
        cum = jnp.dot(lower, log_decay[at], precision=lax.Precision.HIGHEST, preferred_element_type=F32)
        steps.append(step_here)
        cums.append(cum)
        to_end = jnp.exp(cum[SPAN - 1 : SPAN] - cum) * step_here
        b_turned = bs[at].astype(F32).T.astype(BF16)
        decay = []
        for tile in range(tiles):
            columns = slice(tile * TILE, (tile + 1) * TILE)
            weighted = (xs[at, columns].astype(F32) * spread(to_end, tables[tile])).astype(BF16)
            states[span][:, columns] = dot(b_turned, weighted)
            decay.append(spread(jnp.exp(cum[SPAN - 8 :]), tables[tile])[7:8])
        ends.append(decay)

    def hand_on():
        return remote(outgoing, entering, chain_send, chain_recv, {"ctx": me + 1})

    def pass_on(first):
        for tile in range(tiles):
            columns = slice(tile * TILE, (tile + 1) * TILE)
            total = ends[1][tile] * state0[:, columns] + state1[:, columns]
            if not first:
                total = total + ends[0][tile] * ends[1][tile] * entering[:, columns].astype(F32)
            outgoing[:, columns] = total.astype(BF16)
        hand_on().start()

    @pl.when(jnp.logical_not(has_left))
    def _():
        entering[...] = jnp.zeros_like(entering)
        pass_on(True)

    def chain_relay():
        hand_on().wait_recv()

        @pl.when(has_right)
        def _():
            pass_on(False)

    low_lane = lax.broadcasted_iota(jnp.int32, (128, 2 * width), 1) < width
    done = 0
    for span in range(spans):
        base = span * SPAN
        scores = lax.dot_general(
            cs[base : base + SPAN], bs[base : base + SPAN], (((1,), (1,)), ((), ())), preferred_element_type=F32
        )
        scores = jnp.where(causal, scores, 0.0)
        cum = cums[span]
        cum_turned = turned(cum)
        step_turned = turned(steps[span])
        for pair in range(heads // 2):
            columns = slice(pair * 2 * width, (pair + 1) * 2 * width)
            for block in range(2):
                top, reach = block * 128, (block + 1) * 128
                parts = []
                for head in (2 * pair, 2 * pair + 1):
                    gap = cum[top:reach, head : head + 1] - cum_turned[head : head + 1, :reach]
                    mixing = (
                        scores[top:reach, :reach] * jnp.exp(jnp.minimum(gap, 0.0))
                        * step_turned[head : head + 1, :reach]
                    ).astype(BF16)
                    parts.append(dot(mixing, xs[base : base + reach, columns]))
                ssd[base + top : base + reach, columns] = jnp.where(low_lane, parts[0], parts[1])
            done += 1
            if done in (4, 8, 12):

                @pl.when(me == done // 4)
                def _():
                    chain_relay()

            if done in (3, 11):
                next_relay()

    @pl.when(me > 3)
    def _():
        chain_relay()

    next_relay()

    blocks = lambda block, span: nall.at[block, pl.ds(span * SPAN, SPAN)]

    def to_near(span):
        return remote(blocks(p, span), blocks(p, span), tp_send.at[0, span], tp_recv.at[0, span], {"tp": near})

    def to_far(span):
        return remote(blocks(p, span), blocks(p, span), tp_send.at[1, span], tp_recv.at[1, span], {"tp": far})

    def far_to_near(span):
        return remote(blocks(far, span), blocks(far, span), tp_send.at[2, span], tp_recv.at[2, span], {"tp": near})

    skips = [spread(skip_ref[...] + jnp.zeros((8, heads), F32), tables[tile])[0:1] for tile in range(tiles)]
    for span in range(spans):
        at = slice(span * SPAN, (span + 1) * SPAN)
        growth = jnp.exp(cums[span])
        squares = jnp.zeros((SPAN, 1), F32)
        for tile in range(tiles):
            columns = slice(tile * TILE, (tile + 1) * TILE)
            held = entering[:, columns].astype(F32)
            if span == 0:
                carried = dot(cs[at], entering[:, columns])
            else:
                held = ends[0][tile] * held + state0[:, columns]
                high = held.astype(BF16)
                carried = dot(cs[at], high) + dot(cs[at], (held - high.astype(F32)).astype(BF16))
            full = ssd[at, columns] + carried * spread(growth, tables[tile])
            full = full + skips[tile] * xs[at, columns].astype(F32)
            gated = full * silu(z_ref[at, columns].astype(F32))
            ssd[at, columns] = gated
            squares = squares + jnp.sum(gated * gated, axis=1, keepdims=True)
        scale = lax.rsqrt(squares * (1.0 / inner) + EPS)
        for tile in range(tiles):
            columns = slice(tile * TILE, (tile + 1) * TILE)
            gain = gain_ref[:, columns].astype(F32)
            nall[p, at, columns] = (ssd[at, columns] * scale * gain).astype(BF16)
        to_far(span).start()
        to_near(span).start()

    next_relay()
    for span in range(spans):
        to_far(span).wait_recv()
        far_to_near(span).start()
    while events:
        next_relay()
    if n > 4:

        @pl.loop(4, n)
        def _(s):
            for k in range(chunks):
                relay(s, k)

    def settle(s, k):
        for from_left, go, there in ((True, go_right, me - s >= 0), (False, go_left, me + s < n)):

            @pl.when(there)
            def _():
                across(s, k, from_left, other).wait_recv()
                across(s, k, from_left, g).wait_send()

                @pl.when(has_right if from_left else has_left)
                def _():
                    go(s, k).wait_send()

    @pl.when(has_right)
    def _():
        hand_on().wait_send()
        for i in range(3):
            halo(i).wait_send()
        for k in range(chunks):
            go_right(0, k).wait_send()

    @pl.when(has_left)
    def _():
        for k in range(chunks):
            go_left(0, k).wait_send()

    own_copy.wait()
    for span in range(spans):
        to_near(span).wait_recv()
        far_to_near(span).wait_recv()
        to_near(span).wait_send()
        to_far(span).wait_send()
        far_to_near(span).wait_send()
    if n > 4:

        @pl.loop(1, n)
        def _(s):
            for k in range(chunks):
                settle(s, k)
    else:
        for s in range(1, n):
            for k in range(chunks):
                settle(s, k)

    @pl.loop(0, o_ref.shape[1] // TILE)
    def _(tile):
        columns = pl.ds(pl.multiple_of(tile * TILE, TILE), TILE)
        total = dot(nall[0], wfull[0:inner, columns])
        for block in range(1, 4):
            total = total + dot(nall[block], wfull[block * inner : (block + 1) * inner, columns])
        o_ref[:, columns] = total.astype(BF16)


def shards(
    x_in, z_in, b_in, c_in, dt_in, conv_x, conv_bc, dt_bias, a_log, d_skip, norm_gain, out_weight
):
    n = lax.axis_size("ctx")
    rows, inner = x_in.shape
    depth, out_columns = out_weight.shape
    assert lax.axis_size("tp") == 4 and lax.axis_size("groups") == 2
    assert b_in.shape[1] == STATE and rows == 2 * SPAN and conv_x.shape[0] == 4
    chunks = 2 if depth >= 256 else 1
    links = pltpu.SemaphoreType.DMA((n * chunks,))
    vmem = pl.BlockSpec(memory_space=pltpu.VMEM)
    return pl.pallas_call(
        functools.partial(kernel, n, chunks),
        out_shape=jax.ShapeDtypeStruct((rows, out_columns), BF16),
        in_specs=[vmem] * 11 + [pl.BlockSpec(memory_space=pl.ANY)],
        out_specs=vmem,
        scratch_shapes=[
            pltpu.VMEM((n * depth, out_columns), BF16),
            pltpu.VMEM((4, rows, inner), BF16),
            pltpu.VMEM((rows + 8, STATE), F32),
            pltpu.VMEM((rows, inner), BF16),
            pltpu.VMEM((rows, STATE), BF16),
            pltpu.VMEM((rows, STATE), BF16),
            pltpu.VMEM((rows, inner), F32),
            pltpu.VMEM((STATE, inner), F32),
            pltpu.VMEM((STATE, inner), F32),
            pltpu.VMEM((STATE, inner), BF16),
            pltpu.VMEM((STATE, inner), BF16),
            pltpu.VMEM((RIM, inner), BF16),
            pltpu.VMEM((RIM, STATE), BF16),
            pltpu.VMEM((RIM, STATE), BF16),
            pltpu.SemaphoreType.DMA,
            pltpu.SemaphoreType.DMA((3,)),
            pltpu.SemaphoreType.DMA((3,)),
            pltpu.SemaphoreType.DMA,
            pltpu.SemaphoreType.DMA,
        ]
        + [links] * 8
        + [pltpu.SemaphoreType.DMA((3, 2)), pltpu.SemaphoreType.DMA((3, 2))],
        compiler_params=pltpu.CompilerParams(
            collective_id=0, has_side_effects=True, vmem_limit_bytes=48 * 1024 * 1024
        ),
    )(
        x_in, z_in, b_in, c_in, dt_in, conv_x, conv_bc,
        dt_bias[None], a_log[None], d_skip[None], norm_gain[None], out_weight,
    )


def solution(mesh):
    rows = P(("groups", "ctx"), "tp")
    return jax.shard_map(
        shards,
        mesh=mesh,
        in_specs=(
            rows, rows, rows, rows, rows,
            P(None, "tp"), P(None, None, "tp"),
            P("tp"), P("tp"), P("tp"), P("tp"),
            P("ctx", "tp"),
        ),
        out_specs=rows,
        check_vma=False,
    )
```

time: 310 us -> 113 us (0.36); the launches traced: 305 us -> 112 us
  waiting for transfers between devices: 218 us -> 0 us
  Pallas kernels: 0 us -> 100 us
  other arithmetic: 21.4 us -> 0 us
  matrix products: 18.2 us -> 0 us
  between operations: 13.8 us -> 0.03 us
  blocking collectives: 13.3 us -> 0 us
  starting transfers between devices: 3.93 us -> 0 us
  local copies, waits for them, and re-layouts: 14.9 us -> 11.7 us
    all_gather x3 -> x0, waiting for transfers between devices: 217 us -> none  [the longest x1 149 us: shards(): weight_full = lax.all_gather(out_weight, 'ctx', axis=0, tiled=True)]
    pallas_call x0 -> x1, Pallas kernels: none -> 100 us  [shards(): pl.pallas_call(functools.partial(kernel, n, chunks), out_shape=jax.ShapeD...]
    dot_general x10 -> x0, matrix products: 18.2 us -> none  [the longest x1 10.1 us: shards(): mixed = jnp.dot(gathered, weight_full, preferred_element_type=jnp.float32)]
    unnamed x1 -> x0, blocking collectives: 13.3 us -> none
    convert_element_type x6 -> x0, other arithmetic: 9.74 us -> none  [the longest x3 7.65 us: causal_conv(): return jax.nn.silu(summed).astype(jnp.bfloat16)]
    unnamed x12 -> x22, local copies, waits for them, and re-layouts: 1.49 us -> 11 us
    dynamic_slice x8 -> x0, local copies, waits for them, and re-layouts: 5.58 us -> none  [the longest x6 4.29 us: take_rows(): return lax.dynamic_slice_in_dim(array, first_row, SPAN, 0)]
    select_n x4 -> x0, other arithmetic: 4.33 us -> none  [the longest x3 3.52 us: hop(): jnp.where(position < mine, new, old)]
  transfers between devices with their start and end apart: 6 -> 0, of which waited for: 3 -> 0; matrix products, arithmetic and copies ran while one was open for 3% -> 0% of each run, Pallas kernels for 0% -> 0%
where the time goes in v1:
time: 113 us; the launch traced here: 112 us
  Pallas kernels  100 us (88%)
  local copies, waits for them, and re-layouts  11.7 us (10%)
    pallas_call x1, Pallas kernels, shards(): pl.pallas_call(functools.partial(kernel, n, chunks), out_shape=jax.ShapeD...  100 us
    unnamed x22, local copies, waits for them, and re-layouts  11 us

profile of v1, /device:TPU:26, one launch (start us, length us, event | category | flops | bytes accessed | tf_op | source)
XLA Modules:
  0.0 112.2 jit_solution(4051787006056708448)
XLA Ops:
  0.0 0.7 broadcast_in_dim.15.gain_ref
  0.7 0.8 copy.13.dt_ref
  1.5 0.0 copy-start
  1.5 1.6 %copy-done = bf16[1024,1024]{1,0:T(8,128)(2,1)S(1)} copy-done((bf16[1024,1024]{1,0:T(8,128)(2,1)S(1)}, bf16[1024,1024]{1,0:T(8,128)(2,1)}, u32[]{:S(2)}) %copy-start) | copy-done | bytes 2097176
  3.1 0.0 copy-start.1
  3.1 1.2 %copy-done.1 = bf16[512,1024]{1,0:T(8,128)(2,1)S(1)} copy-done((bf16[512,1024]{1,0:T(8,128)(2,1)S(1)}, bf16[512,1024]{1,0:T(8,128)(2,1)}, u32[]{:S(2)}) %copy-start.1) | copy-done | bytes 1048600
  4.3 0.0 copy-start.2
  4.3 1.2 %copy-done.2 = bf16[512,1024]{1,0:T(8,128)(2,1)S(1)} copy-done((bf16[512,1024]{1,0:T(8,128)(2,1)S(1)}, bf16[512,1024]{1,0:T(8,128)(2,1)}, u32[]{:S(2)}) %copy-start.2) | copy-done | bytes 1048600
  5.6 0.0 copy-start.3
  5.6 0.9 copy-done.3
  6.5 0.0 copy-start.4
  6.5 0.9 copy-done.4
  7.4 0.0 copy-start.5
  7.4 0.7 copy-done.5
  8.1 0.0 copy-start.6
  8.1 0.7 copy-done.6
  8.8 0.0 copy-start.7
  8.8 0.7 copy-done.7
  9.4 0.0 copy-start.8
  9.4 0.7 copy-done.8
  10.1 0.0 copy-start.9
  10.1 0.7 copy-done.9
  10.7 100.4 %shard_map.118 = bf16[512,1024]{1,0:T(8,128)(2,1)S(1)} custom-call(bf16[512,1024]{1,0:T(8,128)(2,1)S(1)} %copy-done.1, bf16[512,1024]{1,0:T(8,128)(2,1)S(1)} %copy-done.2, bf16[512,128]{1,0:T(8,128)(2,1)S(1)} %copy-done.3, bf16[512,128]{1,0:T(8,128)(2,1)S(1)} %copy-done.4, bf16[512,16]{1,0:T(8,128)(2,1)S(1)} %copy.13.dt_ref, bf16[4,1024]{1,0:T(4,128)(2,1)S(1)} %copy-done.5, ...), custom_call_target="tpu_custom_call" | custom-call | tf_op jit(solution)/shard_map/pallas_call | solution.py:412
  111.2 1.0 copy.15
Async XLA Ops:
  1.5 1.6 %copy-start = (bf16[1024,1024]{1,0:T(8,128)(2,1)S(1)}, bf16[1024,1024]{1,0:T(8,128)(2,1)}, u32[]{:S(2)}) copy-start(bf16[1024,1024]{1,0:T(8,128)(2,1)} %w_ref.1) | copy-start | bytes 6291460
  3.1 1.2 %copy-start.1 = (bf16[512,1024]{1,0:T(8,128)(2,1)S(1)}, bf16[512,1024]{1,0:T(8,128)(2,1)}, u32[]{:S(2)}) copy-start(bf16[512,1024]{1,0:T(8,128)(2,1)} %x_ref.1) | copy-start | bytes 3145732
  4.3 1.2 %copy-start.2 = (bf16[512,1024]{1,0:T(8,128)(2,1)S(1)}, bf16[512,1024]{1,0:T(8,128)(2,1)}, u32[]{:S(2)}) copy-start(bf16[512,1024]{1,0:T(8,128)(2,1)} %z_ref.1) | copy-start | bytes 3145732
  5.6 0.9 copy-start.3
  6.5 0.9 copy-start.4
  7.4 0.7 copy-start.5
  8.1 0.7 copy-start.6
  8.8 0.7 copy-start.7
  9.4 0.7 copy-start.8
  10.1 0.7 copy-start.9

commit v2 on v1

--- a/solution.py
+++ b/solution.py
@@ -32,8 +32,9 @@
 
 def kernel(
     n, chunks,
-    x_ref, z_ref, b_ref, c_ref, dt_ref, conv_ref, convbc_ref, bias_ref, alog_ref, skip_ref, gain_ref, w_ref,
+    x_hbm, z_hbm, b_hbm, c_hbm, dt_hbm, conv_hbm, convbc_hbm, bias_hbm, alog_hbm, skip_hbm, gain_hbm, w_ref,
     o_ref,
+    x_ref, z_ref, b_ref, c_ref, dt_ref, conv_ref, convbc_ref, bias_ref, alog_ref, skip_ref, gain_ref, in_sem, total_ref,
     wfull, nall, xe, xs, bs, cs, ssd, state0, state1, entering, outgoing, halo_x, halo_b, halo_c,
     own_sem, halo_send, halo_recv, chain_send, chain_recv,
     right_send, right_recv, left_send, left_recv,
@@ -55,6 +56,11 @@
     piece = half // chunks
     has_left, has_right = me > 0, me < n - 1
 
+    sources = (x_hbm, z_hbm, b_hbm, c_hbm, dt_hbm, conv_hbm, convbc_hbm, bias_hbm, alog_hbm, skip_hbm, gain_hbm)
+    held_in = (x_ref, z_ref, b_ref, c_ref, dt_ref, conv_ref, convbc_ref, bias_ref, alog_ref, skip_ref, gain_ref)
+    loads = [
+        pltpu.make_async_copy(source, to, in_sem.at[i]) for i, (source, to) in enumerate(zip(sources, held_in))
+    ]
     barrier = pltpu.get_barrier_semaphore()
     for device in ({"groups": other}, {"tp": near}, {"tp": far}):
         pl.semaphore_signal(barrier, inc=1, device_id=device, device_id_type=MESH)
@@ -67,6 +73,8 @@
     def _():
         pl.semaphore_signal(barrier, inc=1, device_id={"ctx": me + 1}, device_id_type=MESH)
 
+    for load in loads:
+        load.start()
     pl.semaphore_wait(barrier, 3 + has_left.astype(jnp.int32) + has_right.astype(jnp.int32))
 
     def remote(src, dst, send, recv, device):
@@ -75,7 +83,7 @@
         )
 
     def halo(i):
-        src = (x_ref, b_ref, c_ref)[i].at[pl.ds(rows - RIM, RIM)]
+        src = (x_hbm, b_hbm, c_hbm)[i].at[pl.ds(rows - RIM, RIM)]
         dst = (halo_x, halo_b, halo_c)[i]
         return remote(src, dst, halo_send.at[i], halo_recv.at[i], {"ctx": me + 1})
 
@@ -159,6 +167,9 @@
     def next_relay():
         if events:
             relay(*events.pop(0))
+
+    for i in (2, 3, 0, 4, 5, 6, 7, 8):
+        loads[i].wait()
 
     @pl.when(jnp.logical_not(has_left))
     def _():
@@ -231,29 +242,33 @@
             decay.append(spread(jnp.exp(cum[SPAN - 8 :]), tables[tile])[7:8])
         ends.append(decay)
 
-    def hand_on():
-        return remote(outgoing, entering, chain_send, chain_recv, {"ctx": me + 1})
-
-    def pass_on(first):
+    def hand_on(tile):
+        return remote(
+            outgoing.at[tile], entering.at[tile], chain_send.at[tile], chain_recv.at[tile], {"ctx": me + 1}
+        )
+
+    def pass_on(tile, first):
+        columns = slice(tile * TILE, (tile + 1) * TILE)
+        total = ends[1][tile] * state0[:, columns] + state1[:, columns]
+        if not first:
+            total = total + ends[0][tile] * ends[1][tile] * entering[tile].astype(F32)
+        outgoing[tile] = total.astype(BF16)
+        hand_on(tile).start()
+
+    @pl.when(jnp.logical_not(has_left))
+    def _():
+        entering[...] = jnp.zeros_like(entering)
         for tile in range(tiles):
-            columns = slice(tile * TILE, (tile + 1) * TILE)
-            total = ends[1][tile] * state0[:, columns] + state1[:, columns]
-            if not first:
-                total = total + ends[0][tile] * ends[1][tile] * entering[:, columns].astype(F32)
-            outgoing[:, columns] = total.astype(BF16)
-        hand_on().start()
-
-    @pl.when(jnp.logical_not(has_left))
-    def _():
-        entering[...] = jnp.zeros_like(entering)
-        pass_on(True)
-
-    def chain_relay():
-        hand_on().wait_recv()
-
-        @pl.when(has_right)
-        def _():
-            pass_on(False)
+            pass_on(tile, True)
+
+    def chain_relay(tile):
+        @pl.when(has_left)
+        def _():
+            hand_on(tile).wait_recv()
+
+            @pl.when(has_right)
+            def _():
+                pass_on(tile, False)
 
     low_lane = lax.broadcasted_iota(jnp.int32, (128, 2 * width), 1) < width
     done = 0
@@ -280,20 +295,18 @@
                     parts.append(dot(mixing, xs[base : base + reach, columns]))
                 ssd[base + top : base + reach, columns] = jnp.where(low_lane, parts[0], parts[1])
             done += 1
-            if done in (4, 8, 12):
-
-                @pl.when(me == done // 4)
-                def _():
-                    chain_relay()
-
-            if done in (3, 11):
+            if done == 8:
                 next_relay()
 
-    @pl.when(me > 3)
-    def _():
-        chain_relay()
-
     next_relay()
+    for tile in range(tiles):
+        chain_relay(tile)
+        if tile in (1, 2):
+            next_relay()
+
+    loads[1].wait()
+    loads[9].wait()
+    loads[10].wait()
 
     blocks = lambda block, span: nall.at[block, pl.ds(span * SPAN, SPAN)]
 
@@ -313,9 +326,9 @@
         squares = jnp.zeros((SPAN, 1), F32)
         for tile in range(tiles):
             columns = slice(tile * TILE, (tile + 1) * TILE)
-            held = entering[:, columns].astype(F32)
+            held = entering[tile].astype(F32)
             if span == 0:
-                carried = dot(cs[at], entering[:, columns])
+                carried = dot(cs[at], entering[tile])
             else:
                 held = ends[0][tile] * held + state0[:, columns]
                 high = held.astype(BF16)
@@ -333,25 +346,80 @@
         to_far(span).start()
         to_near(span).start()
 
-    next_relay()
+    def settle(s, k):
+        for from_left, there in ((True, me - s >= 0), (False, me + s < n)):
+
+            @pl.when(there)
+            def _():
+                across(s, k, from_left, other).wait_recv()
+
+    def gathered(span):
+        to_near(span).wait_recv()
+        far_to_near(span).wait_recv()
+
+    def multiply(block, first=False):
+        @pl.loop(0, o_ref.shape[1] // TILE)
+        def _(tile):
+            columns = pl.ds(pl.multiple_of(tile * TILE, TILE), TILE)
+            part = dot(nall[block], wfull[pl.ds(pl.multiple_of(block * depth, 16), depth), columns])
+            if first:
+                total_ref[:, columns] = part
+            else:
+                total_ref[:, columns] += part
+
+    def multiply_around(s):
+        for k in range(chunks):
+            settle(s, k)
+
+        @pl.when(me - s >= 0)
+        def _():
+            multiply(me - s)
+
+        @pl.when(me + s < n)
+        def _():
+            multiply(me + s)
+
+    def relays(count):
+        for _ in range(count):
+            next_relay()
+
+    stepwise = depth == inner
+    relays(2)
+    to_far(0).wait_recv()
+    far_to_near(0).start()
+    relays(3)
+    to_far(1).wait_recv()
+    far_to_near(1).start()
+    own_copy.wait()
+    relays(1)
     for span in range(spans):
-        to_far(span).wait_recv()
-        far_to_near(span).start()
-    while events:
-        next_relay()
-    if n > 4:
+        gathered(span)
+    if stepwise:
+        multiply(me, True)
+        multiply_around(1)
+        for s in range(2, n):
+            while events and events[0][0] <= s:
+                next_relay()
+            multiply_around(s)
+    else:
+        while events:
+            next_relay()
 
         @pl.loop(4, n)
         def _(s):
             for k in range(chunks):
                 relay(s, k)
 
-    def settle(s, k):
+        @pl.loop(1, n)
+        def _(s):
+            for k in range(chunks):
+                settle(s, k)
+
+    def sent(s, k):
         for from_left, go, there in ((True, go_right, me - s >= 0), (False, go_left, me + s < n)):
 
             @pl.when(there)
             def _():
-                across(s, k, from_left, other).wait_recv()
                 across(s, k, from_left, g).wait_send()
 
                 @pl.when(has_right if from_left else has_left)
@@ -360,7 +428,8 @@
 
     @pl.when(has_right)
     def _():
-        hand_on().wait_send()
+        for tile in range(tiles):
+            hand_on(tile).wait_send()
         for i in range(3):
             halo(i).wait_send()
         for k in range(chunks):
@@ -371,10 +440,7 @@
         for k in range(chunks):
             go_left(0, k).wait_send()
 
-    own_copy.wait()
     for span in range(spans):
-        to_near(span).wait_recv()
-        far_to_near(span).wait_recv()
         to_near(span).wait_send()
         to_far(span).wait_send()
         far_to_near(span).wait_send()
@@ -383,19 +449,22 @@
         @pl.loop(1, n)
         def _(s):
             for k in range(chunks):
-                settle(s, k)
+                sent(s, k)
     else:
         for s in range(1, n):
             for k in range(chunks):
-                settle(s, k)
+                sent(s, k)
 
     @pl.loop(0, o_ref.shape[1] // TILE)
     def _(tile):
         columns = pl.ds(pl.multiple_of(tile * TILE, TILE), TILE)
-        total = dot(nall[0], wfull[0:inner, columns])
-        for block in range(1, 4):
-            total = total + dot(nall[block], wfull[block * inner : (block + 1) * inner, columns])
-        o_ref[:, columns] = total.astype(BF16)
+        if stepwise:
+            o_ref[:, columns] = total_ref[:, columns].astype(BF16)
+        else:
+            total = dot(nall[0], wfull[0:inner, columns])
+            for block in range(1, 4):
+                total = total + dot(nall[block], wfull[block * inner : (block + 1) * inner, columns])
+            o_ref[:, columns] = total.astype(BF16)
 
 
 def shards(
@@ -406,15 +475,21 @@
     depth, out_columns = out_weight.shape
     assert lax.axis_size("tp") == 4 and lax.axis_size("groups") == 2
     assert b_in.shape[1] == STATE and rows == 2 * SPAN and conv_x.shape[0] == 4
-    chunks = 2 if depth >= 256 else 1
+    chunks = 4 if depth >= 256 else 1
     links = pltpu.SemaphoreType.DMA((n * chunks,))
     vmem = pl.BlockSpec(memory_space=pltpu.VMEM)
+    operands = (
+        x_in, z_in, b_in, c_in, dt_in, conv_x, conv_bc,
+        dt_bias[None], a_log[None], d_skip[None], norm_gain[None],
+    )
     return pl.pallas_call(
         functools.partial(kernel, n, chunks),
         out_shape=jax.ShapeDtypeStruct((rows, out_columns), BF16),
-        in_specs=[vmem] * 11 + [pl.BlockSpec(memory_space=pl.ANY)],
+        in_specs=[pl.BlockSpec(memory_space=pl.ANY)] * 12,
         out_specs=vmem,
-        scratch_shapes=[
+        scratch_shapes=[pltpu.VMEM(operand.shape, operand.dtype) for operand in operands]
+        + [pltpu.SemaphoreType.DMA((len(operands),)), pltpu.VMEM((rows, out_columns), F32)]
+        + [
             pltpu.VMEM((n * depth, out_columns), BF16),
             pltpu.VMEM((4, rows, inner), BF16),
             pltpu.VMEM((rows + 8, STATE), F32),
@@ -424,26 +499,23 @@
             pltpu.VMEM((rows, inner), F32),
             pltpu.VMEM((STATE, inner), F32),
             pltpu.VMEM((STATE, inner), F32),
-            pltpu.VMEM((STATE, inner), BF16),
-            pltpu.VMEM((STATE, inner), BF16),
+            pltpu.VMEM((inner // TILE, STATE, TILE), BF16),
+            pltpu.VMEM((inner // TILE, STATE, TILE), BF16),
             pltpu.VMEM((RIM, inner), BF16),
             pltpu.VMEM((RIM, STATE), BF16),
             pltpu.VMEM((RIM, STATE), BF16),
             pltpu.SemaphoreType.DMA,
             pltpu.SemaphoreType.DMA((3,)),
             pltpu.SemaphoreType.DMA((3,)),
-            pltpu.SemaphoreType.DMA,
-            pltpu.SemaphoreType.DMA,
+            pltpu.SemaphoreType.DMA((inner // TILE,)),
+            pltpu.SemaphoreType.DMA((inner // TILE,)),
         ]
         + [links] * 8
         + [pltpu.SemaphoreType.DMA((3, 2)), pltpu.SemaphoreType.DMA((3, 2))],
         compiler_params=pltpu.CompilerParams(
             collective_id=0, has_side_effects=True, vmem_limit_bytes=48 * 1024 * 1024
         ),
-    )(
-        x_in, z_in, b_in, c_in, dt_in, conv_x, conv_bc,
-        dt_bias[None], a_log[None], d_skip[None], norm_gain[None], out_weight,
-    )
+    )(*operands, out_weight)
 
 
 def solution(mesh):

time: 113 us -> 120 us (1.062)
  Pallas kernels: 100 us -> 108 us
    pallas_call x1, Pallas kernels: 100 us -> 108 us  [shards(): pl.pallas_call(functools.partial(kernel, n, chunks), out_shape=jax.ShapeD...]
where the time goes in v2:
time: 120 us
  Pallas kernels  108 us (90%)
  local copies, waits for them, and re-layouts  11.7 us (10%)
    pallas_call x1, Pallas kernels, shards(): pl.pallas_call(functools.partial(kernel, n, chunks), out_shape=jax.ShapeD...  108 us
    unnamed x22, local copies, waits for them, and re-layouts  11 us

profile of v2, /device:TPU:26, one launch (start us, length us, event | category | flops | bytes accessed | tf_op | source)
XLA Modules:
  0.0 119.9 jit_solution(7824449525625566818)
XLA Ops:
  0.0 0.7 broadcast_in_dim.15.gain_hbm
  0.7 0.8 copy.13.dt_hbm
  1.5 0.0 copy-start
  1.5 1.6 %copy-done = bf16[1024,1024]{1,0:T(8,128)(2,1)S(1)} copy-done((bf16[1024,1024]{1,0:T(8,128)(2,1)S(1)}, bf16[1024,1024]{1,0:T(8,128)(2,1)}, u32[]{:S(2)}) %copy-start) | copy-done | bytes 2097176
  3.1 0.0 copy-start.1
  3.1 1.2 %copy-done.1 = bf16[512,1024]{1,0:T(8,128)(2,1)S(1)} copy-done((bf16[512,1024]{1,0:T(8,128)(2,1)S(1)}, bf16[512,1024]{1,0:T(8,128)(2,1)}, u32[]{:S(2)}) %copy-start.1) | copy-done | bytes 1048600
  4.3 0.0 copy-start.2
  4.3 1.2 %copy-done.2 = bf16[512,1024]{1,0:T(8,128)(2,1)S(1)} copy-done((bf16[512,1024]{1,0:T(8,128)(2,1)S(1)}, bf16[512,1024]{1,0:T(8,128)(2,1)}, u32[]{:S(2)}) %copy-start.2) | copy-done | bytes 1048600
  5.6 0.0 copy-start.3
  5.6 0.9 copy-done.3
  6.5 0.0 copy-start.4
  6.5 0.9 copy-done.4
  7.4 0.0 copy-start.5
  7.4 0.7 copy-done.5
  8.1 0.0 copy-start.6
  8.1 0.7 copy-done.6
  8.8 0.0 copy-start.7
  8.8 0.7 copy-done.7
  9.4 0.0 copy-start.8
  9.4 0.7 copy-done.8
  10.1 0.0 copy-start.9
  10.1 0.7 copy-done.9
  10.7 108.2 %shard_map.118 = bf16[512,1024]{1,0:T(8,128)(2,1)S(1)} custom-call(bf16[512,1024]{1,0:T(8,128)(2,1)S(1)} %copy-done.1, bf16[512,1024]{1,0:T(8,128)(2,1)S(1)} %copy-done.2, bf16[512,128]{1,0:T(8,128)(2,1)S(1)} %copy-done.3, bf16[512,128]{1,0:T(8,128)(2,1)S(1)} %copy-done.4, bf16[512,16]{1,0:T(8,128)(2,1)S(1)} %copy.13.dt_hbm, bf16[4,1024]{1,0:T(4,128)(2,1)S(1)} %copy-done.5, ...), custom_call_target="tpu_custom_call" | custom-call | tf_op jit(solution)/shard_map/pallas_call | solution.py:485
  118.9 1.0 copy.15
Async XLA Ops:
  1.5 1.6 %copy-start = (bf16[1024,1024]{1,0:T(8,128)(2,1)S(1)}, bf16[1024,1024]{1,0:T(8,128)(2,1)}, u32[]{:S(2)}) copy-start(bf16[1024,1024]{1,0:T(8,128)(2,1)} %w_ref.1) | copy-start | bytes 6291460
  3.1 1.2 %copy-start.1 = (bf16[512,1024]{1,0:T(8,128)(2,1)S(1)}, bf16[512,1024]{1,0:T(8,128)(2,1)}, u32[]{:S(2)}) copy-start(bf16[512,1024]{1,0:T(8,128)(2,1)} %x_hbm.1) | copy-start | bytes 3145732
  4.3 1.2 %copy-start.2 = (bf16[512,1024]{1,0:T(8,128)(2,1)S(1)}, bf16[512,1024]{1,0:T(8,128)(2,1)}, u32[]{:S(2)}) copy-start(bf16[512,1024]{1,0:T(8,128)(2,1)} %z_hbm.1) | copy-start | bytes 3145732
  5.6 0.9 copy-start.3
  6.5 0.9 copy-start.4
  7.4 0.7 copy-start.5
  8.1 0.7 copy-start.6
  8.8 0.7 copy-start.7
  9.4 0.7 copy-start.8
  10.1 0.7 copy-start.9

commit v3 on v2

--- a/solution.py
+++ b/solution.py
@@ -48,7 +48,7 @@
     near = p + 1 - 2 * lax.rem(p, 2)
     far = lax.rem(p + 2, 4)
     rows, inner = x_ref.shape
-    heads = dt_ref.shape[1]
+    heads = dt_ref.shape[0]
     width = inner // heads
     spans = rows // SPAN
     depth = w_ref.shape[0]
@@ -126,11 +126,13 @@
         spot = (s - 1) * chunks + k
         return remote(wfull.at[at], wfull.at[at], send.at[spot], recv.at[spot], {"groups": other})
 
+    early = min(2, chunks)
     for k in range(chunks):
-
-        @pl.when(has_right)
-        def _():
-            go_right(0, k).start()
+        if k < early:
+
+            @pl.when(has_right)
+            def _():
+                go_right(0, k).start()
 
         @pl.when(has_left)
         def _():
@@ -141,17 +143,12 @@
     )
     own_copy.start()
 
-    def relay(s, k):
-        @pl.when(me - s >= 0)
-        def _():
-            arrival(s, k, True).wait_recv()
-
-            @pl.when(has_right)
-            def _():
-                go_right(s, k).start()
-
-            across(s, k, True, g).start()
-
+    def onward(s, k):
+        @pl.when(jnp.logical_and(me - s >= 0, has_right))
+        def _():
+            go_right(s, k).start()
+
+    def relay(s, k, hold=False):
         @pl.when(me + s < n)
         def _():
             arrival(s, k, False).wait_recv()
@@ -162,11 +159,23 @@
 
             across(s, k, False, g).start()
 
+        @pl.when(me - s >= 0)
+        def _():
+            arrival(s, k, True).wait_recv()
+            across(s, k, True, g).start()
+
+        if not hold:
+            onward(s, k)
+
     events = [(s, k) for s in range(1, min(n, 4)) for k in range(chunks)]
 
-    def next_relay():
+    held_back = []
+
+    def next_relay(hold=False):
         if events:
-            relay(*events.pop(0))
+            if hold:
+                held_back.append(events[0])
+            relay(*events.pop(0), hold)
 
     for i in (2, 3, 0, 4, 5, 6, 7, 8):
         loads[i].wait()
@@ -201,7 +210,7 @@
         columns = pl.ds(pl.multiple_of(tile * STATE, STATE), STATE)
         conv(x_ref, halo_x, lambda cols: conv_ref[:, cols], xs, columns)
 
-    raw = dt_ref[...].astype(F32) + bias_ref[...]
+    raw = dt_ref[...].astype(F32).T + bias_ref[...]
     step = jnp.maximum(raw, 0.0) + jnp.log1p(jnp.exp(-jnp.abs(raw)))
     log_decay = -jnp.exp(alog_ref[...]) * step
     t_at = lax.broadcasted_iota(jnp.int32, (SPAN, SPAN), 0)
@@ -295,14 +304,20 @@
                     parts.append(dot(mixing, xs[base : base + reach, columns]))
                 ssd[base + top : base + reach, columns] = jnp.where(low_lane, parts[0], parts[1])
             done += 1
-            if done == 8:
-                next_relay()
-
-    next_relay()
+            if done == 12 and early > 1:
+                next_relay(True)
+
     for tile in range(tiles):
         chain_relay(tile)
-        if tile in (1, 2):
-            next_relay()
+    for k in range(early, chunks):
+
+        @pl.when(has_right)
+        def _():
+            go_right(0, k).start()
+
+    for s, k in held_back:
+        onward(s, k)
+    next_relay()
 
     loads[1].wait()
     loads[9].wait()
@@ -319,6 +334,7 @@
     def far_to_near(span):
         return remote(blocks(far, span), blocks(far, span), tp_send.at[2, span], tp_recv.at[2, span], {"tp": near})
 
+    gains, per = gain_ref[...].astype(F32), TILE // 128
     skips = [spread(skip_ref[...] + jnp.zeros((8, heads), F32), tables[tile])[0:1] for tile in range(tiles)]
     for span in range(spans):
         at = slice(span * SPAN, (span + 1) * SPAN)
@@ -341,7 +357,7 @@
         scale = lax.rsqrt(squares * (1.0 / inner) + EPS)
         for tile in range(tiles):
             columns = slice(tile * TILE, (tile + 1) * TILE)
-            gain = gain_ref[:, columns].astype(F32)
+            gain = jnp.concatenate([gains[i : i + 1] for i in range(tile * per, (tile + 1) * per)], axis=1)
             nall[p, at, columns] = (ssd[at, columns] * scale * gain).astype(BF16)
         to_far(span).start()
         to_near(span).start()
@@ -384,7 +400,7 @@
             next_relay()
 
     stepwise = depth == inner
-    relays(2)
+    relays(3)
     to_far(0).wait_recv()
     far_to_near(0).start()
     relays(3)
@@ -479,13 +495,13 @@
     links = pltpu.SemaphoreType.DMA((n * chunks,))
     vmem = pl.BlockSpec(memory_space=pltpu.VMEM)
     operands = (
-        x_in, z_in, b_in, c_in, dt_in, conv_x, conv_bc,
-        dt_bias[None], a_log[None], d_skip[None], norm_gain[None],
+        x_in, z_in, b_in, c_in, dt_in.T, conv_x, conv_bc,
+        dt_bias[None], a_log[None], d_skip[None], norm_gain.reshape(-1, 128),
     )
     return pl.pallas_call(
         functools.partial(kernel, n, chunks),
         out_shape=jax.ShapeDtypeStruct((rows, out_columns), BF16),
-        in_specs=[pl.BlockSpec(memory_space=pl.ANY)] * 12,
+        in_specs=[pl.BlockSpec(memory_space=pltpu.HBM)] * 12,
         out_specs=vmem,
         scratch_shapes=[pltpu.VMEM(operand.shape, operand.dtype) for operand in operands]
         + [pltpu.SemaphoreType.DMA((len(operands),)), pltpu.VMEM((rows, out_columns), F32)]
@@ -513,7 +529,7 @@
         + [links] * 8
         + [pltpu.SemaphoreType.DMA((3, 2)), pltpu.SemaphoreType.DMA((3, 2))],
         compiler_params=pltpu.CompilerParams(
-            collective_id=0, has_side_effects=True, vmem_limit_bytes=48 * 1024 * 1024
+            collective_id=0, has_side_effects=True, vmem_limit_bytes=63 * 1024 * 1024
         ),
     )(*operands, out_weight)
 

time: 120 us -> 97.5 us (0.81)
  Pallas kernels: 108 us -> 95.1 us
  local copies, waits for them, and re-layouts: 11.7 us -> 2.26 us
    pallas_call x1, Pallas kernels: 108 us -> 95.1 us  [shards(): pl.pallas_call(functools.partial(kernel, n, chunks), out_shape=jax.ShapeD...]
    unnamed x22 -> x1, local copies, waits for them, and re-layouts: 11 us -> 2.26 us
where the time goes in v3:
time: 97.5 us; the launch traced here: 97.4 us
  Pallas kernels  95.1 us (98%)
  local copies, waits for them, and re-layouts  2.26 us (2%)
    pallas_call x1, Pallas kernels, shards(): pl.pallas_call(functools.partial(kernel, n, chunks), out_shape=jax.ShapeD...  95.1 us
    unnamed x1, local copies, waits for them, and re-layouts  2.26 us

profile of v3, /device:TPU:26, one launch (start us, length us, event | category | flops | bytes accessed | tf_op | source)
XLA Modules:
  0.0 97.4 jit_solution(2387845994967132554)
XLA Ops:
  0.0 95.1 %shard_map.118 = bf16[512,1024]{1,0:T(8,128)(2,1)} custom-call(bf16[512,1024]{1,0:T(8,128)(2,1)} %x_hbm.1, bf16[512,1024]{1,0:T(8,128)(2,1)} %z_hbm.1, bf16[512,128]{1,0:T(8,128)(2,1)} %b_hbm.1, bf16[512,128]{1,0:T(8,128)(2,1)} %c_hbm.1, bf16[16,512]{1,0:T(8,128)(2,1)} %bitcast.5, bf16[4,1024]{1,0:T(4,128)(2,1)} %conv_hbm.1, bf16[2,4,128]{2,1,0:T(4,128)(2,1)} %convbc_hbm.1, ...), custom_call_target="tpu_custom_call" | custom-call | tf_op jit(solution)/shard_map/pallas_call | solution.py:501
  95.1 2.3 %copy.14 = bf16[512,1024]{1,0:T(8,128)(2,1)} copy(bf16[512,1024]{1,0:T(8,128)(2,1)} %shard_map.118) | data formatting | bytes 2097152

commit v4 on v3

--- a/solution.py
+++ b/solution.py
@@ -126,13 +126,12 @@
         spot = (s - 1) * chunks + k
         return remote(wfull.at[at], wfull.at[at], send.at[spot], recv.at[spot], {"groups": other})
 
-    early = min(2, chunks)
+    early = chunks // 2 + me * (chunks // 4) if chunks > 1 else 1
     for k in range(chunks):
-        if k < early:
-
-            @pl.when(has_right)
-            def _():
-                go_right(0, k).start()
+
+        @pl.when(jnp.logical_and(has_right, k < early))
+        def _():
+            go_right(0, k).start()
 
         @pl.when(has_left)
         def _():
@@ -304,20 +303,21 @@
                     parts.append(dot(mixing, xs[base : base + reach, columns]))
                 ssd[base + top : base + reach, columns] = jnp.where(low_lane, parts[0], parts[1])
             done += 1
-            if done == 12 and early > 1:
+            if done in (6, 9, 12) and chunks > 1:
                 next_relay(True)
 
     for tile in range(tiles):
         chain_relay(tile)
-    for k in range(early, chunks):
-
-        @pl.when(has_right)
+    for k in range(chunks):
+
+        @pl.when(jnp.logical_and(has_right, k >= early))
         def _():
             go_right(0, k).start()
 
     for s, k in held_back:
         onward(s, k)
-    next_relay()
+    for _ in range(3):
+        next_relay()
 
     loads[1].wait()
     loads[9].wait()
@@ -400,14 +400,14 @@
             next_relay()
 
     stepwise = depth == inner
-    relays(3)
+    relays(5)
     to_far(0).wait_recv()
     far_to_near(0).start()
-    relays(3)
+    relays(5)
     to_far(1).wait_recv()
     far_to_near(1).start()
     own_copy.wait()
-    relays(1)
+    relays(3)
     for span in range(spans):
         gathered(span)
     if stepwise:
@@ -491,7 +491,7 @@
     depth, out_columns = out_weight.shape
     assert lax.axis_size("tp") == 4 and lax.axis_size("groups") == 2
     assert b_in.shape[1] == STATE and rows == 2 * SPAN and conv_x.shape[0] == 4
-    chunks = 4 if depth >= 256 else 1
+    chunks = 8 if depth >= 256 else 1
     links = pltpu.SemaphoreType.DMA((n * chunks,))
     vmem = pl.BlockSpec(memory_space=pltpu.VMEM)
     operands = (

time: 97.5 us -> 100 us (1.026)
  Pallas kernels: 95.1 us -> 97.7 us
    pallas_call x1, Pallas kernels: 95.1 us -> 97.7 us  [shards(): pl.pallas_call(functools.partial(kernel, n, chunks), out_shape=jax.ShapeD...]
where the time goes in v4:
time: 100 us
  Pallas kernels  97.7 us (98%)
  local copies, waits for them, and re-layouts  2.26 us (2%)
    pallas_call x1, Pallas kernels, shards(): pl.pallas_call(functools.partial(kernel, n, chunks), out_shape=jax.ShapeD...  97.7 us
    unnamed x1, local copies, waits for them, and re-layouts  2.26 us

profile of v4, /device:TPU:26, one launch (start us, length us, event | category | flops | bytes accessed | tf_op | source)
XLA Modules:
  0.0 100.0 jit_solution(13423050828358774951)
XLA Ops:
  0.0 97.7 %shard_map.118 = bf16[512,1024]{1,0:T(8,128)(2,1)} custom-call(bf16[512,1024]{1,0:T(8,128)(2,1)} %x_hbm.1, bf16[512,1024]{1,0:T(8,128)(2,1)} %z_hbm.1, bf16[512,128]{1,0:T(8,128)(2,1)} %b_hbm.1, bf16[512,128]{1,0:T(8,128)(2,1)} %c_hbm.1, bf16[16,512]{1,0:T(8,128)(2,1)} %bitcast.5, bf16[4,1024]{1,0:T(4,128)(2,1)} %conv_hbm.1, bf16[2,4,128]{2,1,0:T(4,128)(2,1)} %convbc_hbm.1, ...), custom_call_target="tpu_custom_call" | custom-call | tf_op jit(solution)/shard_map/pallas_call | solution.py:501
  97.7 2.3 %copy.14 = bf16[512,1024]{1,0:T(8,128)(2,1)} copy(bf16[512,1024]{1,0:T(8,128)(2,1)} %shard_map.118) | data formatting | bytes 2097152
